TPU v7x, 32 devices: a whole 2x2x4 slice. The times are simulated.
32 devices in a mesh: dp: 8 (over z, y), head: 4 (over x, core).
Axes of the slice: x: 2, y: 2, z: 4, core: 2. Of those that a mesh axis runs over, the one named last changes fastest.
Arguments:
- hidden_in: bfloat16 [2048, 2048], P(('dp', 'head')), may hold values from -6 to 6
- norm_gain: bfloat16 [2048], replicated, may hold values from 0.25 to 1.75
- w_query: bfloat16 [2048, 2048], P(None, 'head'), may hold values from -0.125 to 0.125
- key_weight: bfloat16 [2048, 1024], P(None, 'head'), may hold values from -0.125 to 0.125
- w_value: bfloat16 [2048, 1024], P(None, 'head'), may hold values from -0.125 to 0.125
- query_gain: bfloat16 [128], replicated, may hold values from 0.796875 to 4
- key_gain: bfloat16 [128], replicated, may hold values from 0.25 to 1.75
- w_out: bfloat16 [2048, 2048], P('head'), may hold values from -0.125 to 0.125
- prefix_root_keys: bfloat16 [1024, 1024], P('dp', 'head'), may hold values from -210 to 210
- prefix_root_values: bfloat16 [1024, 1024], P('dp', 'head'), may hold values from -6 to 6
- mid_keys: bfloat16 [4096, 1024], P('dp', 'head'), may hold values from -210 to 210
- mid_values: bfloat16 [4096, 1024], P('dp', 'head'), may hold values from -6 to 6
- mid_lengths: int32 [16], replicated, may hold values from 1 to 256, 2048 in all
- leaf_keys: bfloat16 [4096, 1024], P('dp', 'head'), may hold values from -6 to 6
- leaf_values: bfloat16 [4096, 1024], P('dp', 'head'), may hold values from -6 to 6
- leaf_lengths: int32 [64], P('dp'), may hold values from 1 to 64, 2048 in all
- token_request: int32 [8, 256], P('dp'), may hold values from 0 to 7, never falling along the last dimension, each value on 1 to 64 neighbouring positions
- request_node: int32 [8, 8], P('dp'), may hold values from 0 to 15, as said below
Outputs:
- attn_update: bfloat16 [2048, 2048], P(('dp', 'head'))
- cache_keys: bfloat16 [2048, 1024], P('dp', 'head')
- cache_values: bfloat16 [2048, 1024], P('dp', 'head')
Inputs may be any that keep to these rules, and one draw needn't show every extreme that they name: `token_request`: in each row requests 0 to 7 all occur, in rising order, each on 1 to 64 consecutive tokens; some request has exactly 64. `request_node`: node v is held by dp index v // 2; the 8 requests of one row have parents on 8 different dp indices, one each.
All inputs are finite; a program needn't handle non-finite values. No bound on the sum of `leaf_lengths` on one device may be relied on, other than what follows from the above.
Results may differ from a plain program's by a relative error of at most 0.039.
Values may be sent and summed in bfloat16 or wider, within the bound.
A program may use at most 128 MiB of HBM per device.

v0:
```python
import math

import jax
import jax.numpy as jnp
from jax import lax
from jax.sharding import PartitionSpec as P

MID_DEV = 2
MID_LEN = 256


EPS = 1e-06
THETA = 1000000.0
MASKED = -1e30


def rms_rows(values, gain):
    power = jnp.mean(values * values, axis=-1, keepdims=True)
    return values * lax.rsqrt(power + EPS) * gain


def rotate(values, positions):
    width = values.shape[-1]
    half = width // 2
    exponent = jnp.arange(half).astype(jnp.float32) * (2.0 / width)
    freqs = jnp.power(THETA, -exponent)
    angles = positions.astype(jnp.float32)[:, None] * freqs[None, :]
    cosine = jnp.cos(angles)[:, None, :]
    sine = jnp.sin(angles)[:, None, :]
    first = values[..., :half]
    second = values[..., half:]
    return jnp.concatenate(
        [first * cosine - second * sine, second * cosine + first * sine], axis=-1
    )


def attend_over_block(query_matrix, keys, values, lengths, kv_heads, head_dim):
    blocks, slots, width = query_matrix.shape
    query_group = width // (kv_heads * head_dim)
    span = keys.shape[1]
    heads_query = query_matrix.reshape(blocks, slots, kv_heads, query_group, head_dim)
    key_heads = keys.reshape(blocks, span, kv_heads, head_dim)
    value_heads = values.reshape(blocks, span, kv_heads, head_dim)
    scores = jnp.einsum(
        "bskgd,blkd->bskgl", heads_query, key_heads, preferred_element_type=jnp.float32
    ) / math.sqrt(head_dim)
    live = jnp.arange(span, dtype=jnp.int32)[None, :] < lengths[:, None]
    scores = jnp.where(live[:, None, None, None, :], scores, MASKED)
    highest = jnp.max(scores, axis=-1)
    weights = jnp.exp(scores - highest[..., None])
    total = jnp.sum(weights, axis=-1)
    summed = jnp.einsum(
        "bskgl,blkd->bskgd",
        weights.astype(jnp.bfloat16),
        value_heads,
        preferred_element_type=jnp.float32,
    )
    output = (summed / total[..., None]).astype(jnp.bfloat16).reshape(blocks, slots, width)
    log_total = (highest + jnp.log(total)).reshape(blocks, slots, kv_heads * query_group)
    return (output, log_total)


def body(
    hidden_in,
    norm_gain,
    w_query,
    key_weight,
    w_value,
    query_gain,
    key_gain,
    w_out,
    prefix_root_keys,
    prefix_root_values,
    mid_keys,
    mid_values,
    mid_lengths,
    leaf_keys,
    leaf_values,
    leaf_lengths,
    token_request,
    request_node,
):
    head_dim = query_gain.shape[0]
    query_width = w_query.shape[1]
    key_width = key_weight.shape[1]
    kv_heads = key_width // head_dim
    query_group = query_width // key_width
    scale = 1.0 / math.sqrt(head_dim)
    dp_count = lax.axis_size("dp")
    normalized_input = rms_rows(
        hidden_in.astype(jnp.float32), norm_gain.astype(jnp.float32)
    ).astype(jnp.bfloat16)
    piece = lax.all_gather(normalized_input, "head", axis=0, tiled=True)
    mixed = jnp.concatenate(
        [
            jnp.dot(piece, w_query, preferred_element_type=jnp.float32),
            jnp.dot(piece, key_weight, preferred_element_type=jnp.float32),
            jnp.dot(piece, w_value, preferred_element_type=jnp.float32),
        ],
        axis=1,
    )
    height = mixed.shape[0]
    segment = token_request[0]
    branch_nodes = request_node[0]
    requests = branch_nodes.shape[0]
    request_ids = jnp.arange(requests, dtype=jnp.int32)
    token_ids = jnp.arange(height, dtype=jnp.int32)
    member = segment[None, :] == request_ids[:, None]
    counts = jnp.sum(member.astype(jnp.int32), axis=1)
    starts = jnp.cumsum(counts) - counts
    offset = token_ids - jnp.sum(jnp.where(member, starts[:, None], 0), axis=0)
    node_total = mid_lengths.shape[0]
    node_match = branch_nodes[:, None] == jnp.arange(node_total, dtype=jnp.int32)[None, :]
    branch_length = jnp.sum(jnp.where(node_match, mid_lengths[None, :], 0), axis=1)
    root_total = prefix_root_keys.shape[0] * dp_count
    positions = (
        root_total
        + jnp.sum(jnp.where(member, (branch_length + leaf_lengths)[:, None], 0), axis=0)
        + offset
    )
    query_part = mixed[:, :query_width].reshape(height, query_width // head_dim, head_dim)
    key_portion = mixed[:, query_width : query_width + key_width].reshape(
        height, kv_heads, head_dim
    )
    query_matrix = rotate(rms_rows(query_part, query_gain.astype(jnp.float32)), positions).astype(
        jnp.bfloat16
    )
    new_keys = rotate(rms_rows(key_portion, key_gain.astype(jnp.float32)), positions).astype(
        jnp.bfloat16
    )
    new_values = mixed[:, query_width + key_width :].astype(jnp.bfloat16)
    heads_query = query_matrix.reshape(height, kv_heads, query_group, head_dim)
    query_rows = query_matrix.reshape(height, query_width)
    capacity = 2 * height // dp_count
    slot_ids = jnp.arange(capacity, dtype=jnp.int32)
    req_valid = slot_ids[None, :] < counts[:, None]
    req_picks = jnp.where(req_valid, starts[:, None] + slot_ids[None, :], 0).reshape(-1)
    req_queries = jnp.take(query_rows, req_picks, axis=0).reshape(
        requests, capacity, kv_heads, query_group, head_dim
    )
    req_keys = jnp.take(new_keys, req_picks, axis=0).reshape(requests, capacity, kv_heads, head_dim)
    req_values = jnp.take(new_values, req_picks, axis=0).reshape(
        requests, capacity, kv_heads, head_dim
    )
    leaf_each = leaf_keys.shape[0] // requests
    leaf_heads_key = leaf_keys.reshape(requests, leaf_each, kv_heads, head_dim)
    leaf_heads_value = leaf_values.reshape(requests, leaf_each, kv_heads, head_dim)
    own_live = (slot_ids[None, :] <= slot_ids[:, None])[None, :, :] & req_valid[:, None, :]
    leaf_live = jnp.arange(leaf_each, dtype=jnp.int32)[None, :] < leaf_lengths[:, None]
    own_scores = (
        jnp.einsum("rskgd,rlkd->rskgl", req_queries, req_keys, preferred_element_type=jnp.float32)
        * scale
    )
    leaf_scores = (
        jnp.einsum(
            "rskgd,rlkd->rskgl", req_queries, leaf_heads_key, preferred_element_type=jnp.float32
        )
        * scale
    )
    own_mask = own_live[:, :, None, None, :]
    leaf_mask = leaf_live[:, None, None, None, :]
    own_scores = jnp.where(own_mask, own_scores, MASKED)
    leaf_scores = jnp.where(leaf_mask, leaf_scores, MASKED)
    req_top = jnp.maximum(jnp.max(own_scores, axis=-1), jnp.max(leaf_scores, axis=-1))
    own_weights = jnp.where(own_mask, jnp.exp(own_scores - req_top[..., None]), 0.0)
    leaf_weights = jnp.where(leaf_mask, jnp.exp(leaf_scores - req_top[..., None]), 0.0)
    req_total = jnp.sum(own_weights, axis=-1) + jnp.sum(leaf_weights, axis=-1)
    req_summed = jnp.einsum(
        "rskgl,rlkd->rskgd",
        own_weights.astype(jnp.bfloat16),
        req_values,
        preferred_element_type=jnp.float32,
    )
    req_summed = req_summed + jnp.einsum(
        "rskgl,rlkd->rskgd",
        leaf_weights.astype(jnp.bfloat16),
        leaf_heads_value,
        preferred_element_type=jnp.float32,
    )
    token_slot = jnp.sum(jnp.where(member, (request_ids * capacity)[:, None], 0), axis=0) + offset
    highest = jnp.take(
        req_top.reshape(requests * capacity, kv_heads, query_group), token_slot, axis=0
    )
    total = jnp.take(
        req_total.reshape(requests * capacity, kv_heads, query_group), token_slot, axis=0
    )
    summed = jnp.take(
        req_summed.reshape(requests * capacity, kv_heads, query_group, head_dim), token_slot, axis=0
    )
    piece = (
        lax.all_gather(prefix_root_keys, "dp", axis=0, tiled=True),
        lax.all_gather(prefix_root_values, "dp", axis=0, tiled=True),
    )
    running = total
    gathered = summed
    key_piece = piece[0].reshape(-1, kv_heads, head_dim)
    value_piece = piece[1].reshape(-1, kv_heads, head_dim)
    scores = (
        jnp.einsum("tkgd,skd->tkgs", heads_query, key_piece, preferred_element_type=jnp.float32)
        * scale
    )
    new_top = jnp.maximum(highest, jnp.max(scores, axis=-1))
    shrink = jnp.exp(highest - new_top)
    weights = jnp.exp(scores - new_top[..., None])
    running = running * shrink + jnp.sum(weights, axis=-1)
    gathered = gathered * shrink[..., None] + jnp.einsum(
        "tkgs,skd->tkgd",
        weights.astype(jnp.bfloat16),
        value_piece,
        preferred_element_type=jnp.float32,
    )
    owner_of = branch_nodes // MID_DEV
    owner_ids = jnp.arange(dp_count, dtype=jnp.int32)
    owner_match = owner_of[None, :] == owner_ids[:, None]
    block_start = jnp.sum(jnp.where(owner_match, starts[None, :], 0), axis=1)
    block_count = jnp.sum(jnp.where(owner_match, counts[None, :], 0), axis=1)
    block_slot = jnp.sum(jnp.where(owner_match, (branch_nodes % MID_DEV)[None, :], 0), axis=1)
    block_length = jnp.sum(jnp.where(owner_match, branch_length[None, :], 0), axis=1)
    valid = slot_ids[None, :] < block_count[:, None]
    picks = jnp.where(valid, block_start[:, None] + slot_ids[None, :], 0).reshape(-1)
    query_buffer = jnp.take(query_rows, picks, axis=0).reshape(dp_count, capacity, query_width)
    query_buffer = jnp.where(valid[..., None], query_buffer, jnp.zeros((), jnp.bfloat16))
    wanted = lax.all_to_all(block_slot[:, None], "dp", split_axis=0, concat_axis=0, tiled=True)[
        :, 0
    ]
    own_keys = mid_keys.reshape(MID_DEV, MID_LEN, key_width)
    own_values = mid_values.reshape(MID_DEV, MID_LEN, key_width)
    sent_keys = jnp.take(own_keys, wanted, axis=0)
    sent_values = jnp.take(own_values, wanted, axis=0)
    got_keys, got_values = (
        lax.all_to_all(sent_keys, "dp", split_axis=0, concat_axis=0, tiled=True),
        lax.all_to_all(sent_values, "dp", split_axis=0, concat_axis=0, tiled=True),
    )
    middle_output, middle_log_sum = attend_over_block(
        query_buffer, got_keys, got_values, block_length, kv_heads, head_dim
    )
    flattened_rows = jnp.sum(jnp.where(member, (owner_of * capacity)[:, None], 0), axis=0) + offset
    middle_rows = (
        jnp.take(middle_output.reshape(dp_count * capacity, query_width), flattened_rows, axis=0)
        .astype(jnp.float32)
        .reshape(height, kv_heads, query_group, head_dim)
    )
    middle_maximum = jnp.take(
        middle_log_sum.reshape(dp_count * capacity, kv_heads * query_group), flattened_rows, axis=0
    ).reshape(height, kv_heads, query_group)
    joint = jnp.maximum(new_top, middle_maximum)
    near_part = jnp.exp(new_top - joint)
    far_part = jnp.exp(middle_maximum - joint)
    attn = (near_part[..., None] * gathered + far_part[..., None] * middle_rows) / (
        near_part * running + far_part
    )[..., None]
    attn = attn.reshape(height, query_width).astype(jnp.bfloat16)
    update = lax.psum_scatter(
        jnp.dot(attn, w_out, preferred_element_type=jnp.float32).astype(jnp.bfloat16),
        "head",
        scatter_dimension=0,
        tiled=True,
    )
    return (update, new_keys.reshape(height, key_width), new_values)


def solution(mesh):
    in_specs = (
        P(("dp", "head"), None),
        P(),
        P(None, "head"),
        P(None, "head"),
        P(None, "head"),
        P(),
        P(),
        P("head", None),
        P("dp", "head"),
        P("dp", "head"),
        P("dp", "head"),
        P("dp", "head"),
        P(),
        P("dp", "head"),
        P("dp", "head"),
        P("dp"),
        P("dp", None),
        P("dp", None),
    )
    out_specs = (P(("dp", "head"), None), P("dp", "head"), P("dp", "head"))
    return jax.shard_map(body, mesh=mesh, in_specs=in_specs, out_specs=out_specs, check_vma=False)
```

profile of v0, /device:TPU:9, one launch (start us, length us, event | category | flops | bytes accessed | tf_op | source)
XLA Modules:
  0.0 223.9 jit_solution(1173646855730605797)
XLA Ops:
  11.3 5.7 %all-to-all-start = ((s32[8,1,1]{2,1,0:T(1,128)}), s32[8,1,1]{2,1,0:T(1,128)S(1)}, u32[]{:S(2)}, u32[]{:S(2)}) async-start(s32[8,1,1]{2,1,0:T(1,128)} %copy.295), calls=%async_computation | async-start | bytes 8192 | tf_op jit(solution)/shard_map/all_to_all | solution.py:223
  34.6 23.4 %all_gather.10 = bf16[1024,256]{0,1:T(8,128)(2,1)} all-gather(bf16[128,256]{0,1:T(8,128)(2,1)S(1)} %copy.293), channel_id=1, replica_groups=mesh['dp'=8,'head'=4] {'dp'}, dimensions={0}, use_global_device_ids=true | all-gather | bytes 589824 | tf_op jit(solution)/shard_map/all_gather | solution.py:191
  59.5 23.2 %all_gather.11 = bf16[1024,256]{1,0:T(8,128)(2,1)S(1)} all-gather(bf16[128,256]{1,0:T(8,128)(2,1)S(1)} %copy-done.17), channel_id=1, replica_groups=mesh['dp'=8,'head'=4] {'dp'}, dimensions={0}, use_global_device_ids=true | all-gather | bytes 589824 | tf_op jit(solution)/shard_map/all_gather | solution.py:192
  86.4 2.6 %gather_fusion.7 = bf16[8,256,256]{2,1,0:T(8,128)(2,1)} fusion(bf16[2,256,256]{2,1,0:T(8,128)(2,1)} %bitcast.146, s32[1024]{0:T(1024)S(1)} %pad_clamp_fusion.3), kind=kCustom, calls=%fused_computation.2.clone | custom fusion | bytes 2097184 | tf_op jit(solution)/shard_map/jit(_take)/gather | solution.py:228
  89.0 2.8 %broadcast_select_fusion = (bf16[8,256,256]{2,1,0:T(8,128)(2,1)}, bf16[8,256,256]{2,1,0:T(8,128)(2,1)}) fusion(bf16[8,256,256]{2,1,0:T(8,128)(2,1)S(1)} %gather_fusion.9, pred[8]{0:T(512)(128)(4,1)S(1)} %compare_and_fusion.2, bf16[8,256,256]{2,1,0:T(8,128)(2,1)} %gather_fusion.7), kind=kLoop, calls=%fused_computation.48 | loop fusion | flops 1048576 | bytes 4194312 | tf_op jit(solution)/shard_map/jit(_take)/select_n | solution.py:229
  91.8 7.8 %all-to-all-start.1 = ((bf16[8,256,256]{2,1,0:T(8,128)(2,1)}), bf16[8,256,256]{2,1,0:T(8,128)(2,1)}, u32[]{:S(2)}, u32[]{:S(2)}) async-start(bf16[8,256,256]{2,1,0:T(8,128)(2,1)} %get-tuple-element.34), calls=%async_computation.1 | async-start | bytes 2097152 | tf_op jit(solution)/shard_map/all_to_all | solution.py:231
  99.6 2.6 %fusion.89 = f32[256,512]{1,0:T(8,128)S(1)} fusion(bf16[256,2048]{1,0:T(8,128)(2,1)} %all-gather.2.cloned.1.call-done, bf16[2048,512]{1,0:T(8,128)(2,1)} %param.26), kind=kOutput, calls=%fused_computation.188 | convolution fusion | flops 536870912 | bytes 3670016 | tf_op jit(solution)/shard_map/dot_general | solution.py:96
  106.7 2.6 %gather_fusion.2 = bf16[512,256]{1,0:T(8,128)(2,1)} fusion(bf16[256,256]{1,0:T(8,128)(2,1)S(1)} %convolution_convert_fusion.1, s32[1024]{0:T(1024)S(1)} %pad_clamp_fusion.6), kind=kCustom, calls=%fused_computation.8 | custom fusion | bytes 526336 | tf_op jit(solution)/shard_map/jit(_take)/gather | solution.py:142
  111.0 2.5 %multiply_reduce_fusion.1 = (f32[256,2]{0,1:T(2,128)S(1)}, f32[256,256]{0,1:T(8,128)}) fusion(bf16[256,2048]{1,0:T(8,128)(2,1)S(1)} %copy-done.5, bf16[2048,256]{1,0:T(8,128)(2,1)} %param.27), kind=kOutput, calls=%fused_computation.97 | convolution fusion | flops 268566016 | bytes 2361344 | tf_op jit(solution)/shard_map/dot_general | solution.py:97
  116.0 2.1 gather_fusion
  118.2 2.0 gather_fusion.8
  121.1 2.0 reshape.517
  123.2 2.0 gather_fusion.5
  127.5 2.6 %fusion.88 = (f32[8,64,2,2]{1,3,2,0:T(2,128)S(1)}, f32[8,64,2,2,64]{1,4,3,2,0:T(8,128)}) fusion(bf16[8,64,2,128,1]{3,2,1,0,4:T(2,128)(2,1)} %bitcast.161, bf16[8,64,2,2,128]{4,3,2,1,0:T(2,128)(2,1)S(1)} %reshape.512, pred[8,64]{1,0:T(8,128)(4,1)S(1)} %copy-done.21), kind=kOutput, calls=%fused_computation.187 | convolution fusion | flops 33945600 | bytes 1319424 | tf_op jit(solution)/shard_map/rskgd,rlkd->rskgl/dot_general | solution.py:155
  136.7 3.4 %gather_fusion.3 = f32[256,2,2,128]{3,2,1,0:T(2,128)} fusion(f32[512,2,2,128]{3,2,1,0:T(2,128)} %copy.309, s32[1024]{0:T(1024)} %pad_clamp_fusion), kind=kCustom, calls=%fused_computation.9 | custom fusion | bytes 1049600 | tf_op jit(solution)/shard_map/jit(_take)/gather | solution.py:187
  140.1 2.0 copy.310
  142.1 5.4 %all-to-all-start.2 = ((bf16[8,256,256]{2,1,0:T(8,128)(2,1)}), bf16[8,256,256]{2,1,0:T(8,128)(2,1)}, u32[]{:S(2)}, u32[]{:S(2)}) async-start(bf16[8,256,256]{2,1,0:T(8,128)(2,1)} %get-tuple-element.33), calls=%async_computation.2 | async-start | bytes 2097152 | tf_op jit(solution)/shard_map/all_to_all | solution.py:232
  147.5 1.8 fusion.42
  149.7 1.8 gather_fusion.10
  152.6 2.2 gather_fusion.6
  156.7 1.9 copy-done.2
  166.5 3.2 %fusion.16 = bf16[8,64,2,2,128]{4,1,3,2,0:T(8,128)(2,1)} fusion(bf16[8,256,2,128,1]{1,3,4,2,0:T(8,128)(2,1)S(1)} %bitcast.158, f32[8,2,256,64,2]{2,3,4,1,0:T(8,128)} %copy-done.7, f32[8,64,2,2]{1,3,2,0:T(2,128)S(1)} %get-tuple-element.47, pred[8,256]{1,0:T(8,128)(4,1)S(1)} %copy-done.19, f32[8,64,2,2]{1,3,2,0:T(2,128)S(1)} %fusion.9), kind=kOutput, calls=%fused_computation.37 | convolution fusion | flops 136839168 | bytes 3688448 | tf_op jit(solution)/shard_map/bskgl,blkd->bskgd/dot_general | solution.py:52
  173.9 3.5 %fusion.37 = bf16[256,2,2,128]{0,3,2,1:T(8,128)(2,1)S(1)} fusion(bf16[1024,2,128,1]{0,2,3,1:T(8,128)(2,1)} %bitcast.160, f32[2,256,2,1024]{3,1,2,0:T(8,128)} %copy-done.2, f32[256,2,2]{0,2,1:T(2,128)S(1)} %fusion.74, f32[256,2,2,128]{0,3,2,1:T(8,128)} %copy.310, f32[256,2,2]{0,2,1:T(2,128)S(1)} %get-tuple-element.16, ...), kind=kOutput, calls=%fused_computation.52 | convolution fusion | flops 272891904 | bytes 5788160 | tf_op jit(solution)/shard_map/tkgs,skd->tkgd/dot_general | solution.py:206
  179.9 37.2 %reduce-scatter.2.cloned.1.call-done = bf16[64,2048]{1,0:T(8,128)(2,1)} async-done(((bf16[256,2048]{1,0:T(8,128)(2,1)}), bf16[64,2048]{1,0:T(8,128)(2,1)}) %reduce-scatter.2.cloned.1.call-update) | async-done | bytes 262160 | tf_op jit(solution)/shard_map/reduce_scatter | solution.py:253
  (176 shorter events, 62.8 us)
Async XLA Ops:
  7.2 170.3 %copy-start = (bf16[512,2048]{1,0:T(8,128)(2,1)S(1)}, bf16[512,2048]{1,0:T(8,128)(2,1)}, u32[]{:S(2)}) copy-start(bf16[512,2048]{1,0:T(8,128)(2,1)} %param.31) | copy-start | bytes 6291460
  7.2 26.7 %copy-start.16 = (bf16[512,256]{1,0:T(8,128)(2,1)S(1)}, bf16[512,256]{1,0:T(8,128)(2,1)}, u32[]{:S(2)}) copy-start(bf16[512,256]{1,0:T(8,128)(2,1)} %param.38) | copy-start | bytes 786436
  7.2 52.3 %copy-start.17 = (bf16[128,256]{1,0:T(8,128)(2,1)S(1)}, bf16[128,256]{1,0:T(8,128)(2,1)}, u32[]{:S(2)}) copy-start(bf16[128,256]{1,0:T(8,128)(2,1)} %param.33) | copy-start | bytes 196612
  11.3 73.6 %all-to-all-start = ((s32[8,1,1]{2,1,0:T(1,128)}), s32[8,1,1]{2,1,0:T(1,128)S(1)}, u32[]{:S(2)}, u32[]{:S(2)}) async-start(s32[8,1,1]{2,1,0:T(1,128)} %copy.295), calls=%async_computation | async-start | bytes 8192 | tf_op jit(solution)/shard_map/all_to_all | solution.py:223
  17.1 82.6 %all-gather.2.cloned.1.call-start = ((), (), s32[]{:S(2)}) async-start(), calls=%async_computation.4 | async-start | bytes 1310720 | tf_op jit(solution)/shard_map/all_gather | solution.py:93
  20.7 65.1 %copy-start.3 = (bf16[512,256]{1,0:T(8,128)(2,1)S(1)}, bf16[512,256]{1,0:T(8,128)(2,1)}, u32[]{:S(2)}) copy-start(bf16[512,256]{1,0:T(8,128)(2,1)} %param.35) | copy-start | bytes 786436
  86.4 2.6 %copy-start.29 = (s32[8]{0:T(128)S(1)}, s32[8]{0:T(128)}, u32[]{:S(2)}) copy-start(s32[8]{0:T(128)} %copy-done.28) | copy-start | bytes 100
  91.8 50.3 %all-to-all-start.1 = ((bf16[8,256,256]{2,1,0:T(8,128)(2,1)}), bf16[8,256,256]{2,1,0:T(8,128)(2,1)}, u32[]{:S(2)}, u32[]{:S(2)}) async-start(bf16[8,256,256]{2,1,0:T(8,128)(2,1)} %get-tuple-element.34), calls=%async_computation.1 | async-start | bytes 2097152 | tf_op jit(solution)/shard_map/all_to_all | solution.py:231
  99.6 3.2 %copy-start.27 = (f32[128]{0:T(128)S(1)}, f32[128]{0:T(128)}, u32[]{:S(2)}) copy-start(f32[128]{0:T(128)} %convert_element_type.86) | copy-start | bytes 1540
  103.2 3.1 %copy-start.5 = (bf16[256,2048]{1,0:T(8,128)(2,1)S(1)}, bf16[256,2048]{1,0:T(8,128)(2,1)}, u32[]{:S(2)}) copy-start(bf16[256,2048]{1,0:T(8,128)(2,1)} %all-gather.2.cloned.1.call-done) | copy-start | bytes 3145732
  103.2 3.1 %copy-start.13 = (bf16[2048,256]{1,0:T(8,128)(2,1)S(1)}, bf16[2048,256]{1,0:T(8,128)(2,1)}, u32[]{:S(2)}) copy-start(bf16[2048,256]{1,0:T(8,128)(2,1)} %param.28) | copy-start | bytes 3145732
  106.7 6.8 %copy-start.1 = (bf16[256,256]{1,0:T(8,128)(2,1)}, bf16[256,256]{1,0:T(8,128)(2,1)S(1)}, u32[]{:S(2)}) copy-start(bf16[256,256]{1,0:T(8,128)(2,1)S(1)} %convolution_convert_fusion.1) | copy-start | bytes 393220
  109.3 5.5 %copy-start.30 = (f32[128]{0:T(128)S(1)}, f32[128]{0:T(128)}, u32[]{:S(2)}) copy-start(f32[128]{0:T(128)} %convert_element_type.82) | copy-start | bytes 1540
  113.5 4.7 %copy-start.12 = (bf16[256,4,128]{2,1,0:T(4,128)(2,1)S(1)}, bf16[256,4,128]{2,1,0:T(4,128)(2,1)}, u32[]{:S(2)}) copy-start(bf16[256,4,128]{2,1,0:T(4,128)(2,1)} %pad_maximum_fusion) | copy-start | bytes 786436
  125.1 2.2 copy-start.11
  125.2 2.2 copy-start.23
  125.2 2.3 %copy-start.21 = (pred[8,64]{1,0:T(8,128)(4,1)S(1)}, pred[8,64]{1,0:T(8,128)(4,1)}, u32[]{:S(2)}) copy-start(pred[8,64]{1,0:T(8,128)(4,1)} %iota_compare_fusion.5) | copy-start | bytes 1540
  127.3 2.8 %copy-start.15 = (bf16[8,64,2,2,128]{4,3,2,1,0:T(2,128)(2,1)}, bf16[8,64,2,2,128]{4,3,2,1,0:T(2,128)(2,1)S(1)}, u32[]{:S(2)}) copy-start(bf16[8,64,2,2,128]{4,3,2,1,0:T(2,128)(2,1)S(1)} %reshape.512) | copy-start | bytes 1572868
  127.3 2.8 %copy-start.14 = (pred[8,64,64]{1,2,0:T(8,128)(4,1)S(1)}, pred[8,64,64]{1,2,0:T(8,128)(4,1)}, u32[]{:S(2)}) copy-start(pred[8,64,64]{1,2,0:T(8,128)(4,1)} %broadcast_and_fusion) | copy-start | bytes 98308
  142.1 22.9 %all-to-all-start.2 = ((bf16[8,256,256]{2,1,0:T(8,128)(2,1)}), bf16[8,256,256]{2,1,0:T(8,128)(2,1)}, u32[]{:S(2)}, u32[]{:S(2)}) async-start(bf16[8,256,256]{2,1,0:T(8,128)(2,1)} %get-tuple-element.33), calls=%async_computation.2 | async-start | bytes 2097152 | tf_op jit(solution)/shard_map/all_to_all | solution.py:232
  147.5 7.3 %copy-start.10 = (bf16[256,4,64]{2,0,1:T(8,128)(2,1)S(1)}, bf16[256,4,64]{2,0,1:T(8,128)(2,1)}, u32[]{:S(2)}) copy-start(bf16[256,4,64]{2,0,1:T(8,128)(2,1)} %copy.291) | copy-start | bytes 393220
  147.5 69.5 %reduce-scatter.2.cloned.1.call-start = ((), (), s32[]{:S(2)}) async-start(), calls=%async_computation.5 | async-start | bytes 1310720 | tf_op jit(solution)/shard_map/reduce_scatter | solution.py:253
  149.4 5.5 %copy-start.6 = (bf16[1024,256]{0,1:T(8,128)(2,1)S(1)}, bf16[1024,256]{0,1:T(8,128)(2,1)}, u32[]{:S(2)}) copy-start(bf16[1024,256]{0,1:T(8,128)(2,1)} %all_gather.10) | copy-start | bytes 1572868
  171.6 2.3 %copy-start.24 = (pred[256]{0:T(512)(128)(4,1)S(1)}, pred[256]{0:T(512)(128)(4,1)}, u32[]{:S(2)}) copy-start(pred[256]{0:T(512)(128)(4,1)} %get-tuple-element.28) | copy-start | bytes 772
  (13 other events, 19.5 us)
Sparse Core Ops, SparseCore 0:
  20.8 18.5 all-gather.1
  179.3 37.7 reduce-scatter.1
where the time goes:
time: 227 us; the launch traced here: 224 us
  local copies, waits for them, and re-layouts  50.7 us (22%)
  blocking collectives  46.6 us (21%)
  waiting for transfers between devices  37.2 us (16%)
  other arithmetic  32.2 us (14%)
  matrix products  23.6 us (10%)
  starting transfers between devices  19 us (8%)
  between operations  14.7 us (6%)
    reduce_scatter x1, waiting for transfers between devices, body(): lax.psum_scatter(jnp.dot(attn, w_out, preferred_element_type=jnp.float32)...  37.2 us
    all_gather x1, blocking collectives, body(): lax.all_gather(prefix_root_keys, 'dp', axis=0, tiled=True)  23.4 us
    all_gather x1, blocking collectives, body(): lax.all_gather(prefix_root_values, 'dp', axis=0, tiled=True)  23.2 us
    all_to_all x1, starting transfers between devices, body(): lax.all_to_all(sent_keys, 'dp', split_axis=0, concat_axis=0, tiled=True)  7.79 us
    all_to_all x1, starting transfers between devices, body(): lax.all_to_all(block_slot[:, None], 'dp', split_axis=0, concat_axis=0, ti...  5.72 us
    unnamed x67, local copies, waits for them, and re-layouts  5.58 us
    all_to_all x1, starting transfers between devices, body(): lax.all_to_all(sent_values, 'dp', split_axis=0, concat_axis=0, tiled=True)  5.44 us
    gather x2, local copies, waits for them, and re-layouts, body(): jnp.take(req_summed.reshape(requests * capacity, kv_heads, query_group, h...  5.41 us
  transfers between devices with their start and end apart: 5, of which 1 were waited for; matrix products, arithmetic and copies ran while one was open for 38% of the time, Pallas kernels for 0%

commit v1 on v0

v1 whole, which is shorter than its diff:
```python
import math

import jax
import jax.numpy as jnp
from jax import lax
from jax.sharding import PartitionSpec as P

MID_DEV = 2
MID_LEN = 256


EPS = 1e-06
THETA = 1000000.0
MASKED = -1e30


def rms_rows(values, gain):
    power = jnp.mean(values * values, axis=-1, keepdims=True)
    return values * lax.rsqrt(power + EPS) * gain


def rotate(values, positions):
    width = values.shape[-1]
    half = width // 2
    exponent = jnp.arange(half).astype(jnp.float32) * (2.0 / width)
    freqs = jnp.power(THETA, -exponent)
    angles = positions.astype(jnp.float32)[:, None] * freqs[None, :]
    cosine = jnp.cos(angles)[:, None, :]
    sine = jnp.sin(angles)[:, None, :]
    first = values[..., :half]
    second = values[..., half:]
    return jnp.concatenate(
        [first * cosine - second * sine, second * cosine + first * sine], axis=-1
    )


def body(
    hidden_in,
    norm_gain,
    w_query,
    key_weight,
    w_value,
    query_gain,
    key_gain,
    w_out,
    prefix_root_keys,
    prefix_root_values,
    mid_keys,
    mid_values,
    mid_lengths,
    leaf_keys,
    leaf_values,
    leaf_lengths,
    token_request,
    request_node,
):
    head_dim = query_gain.shape[0]
    query_width = w_query.shape[1]
    key_width = key_weight.shape[1]
    kv_heads = key_width // head_dim
    query_group = query_width // key_width
    scale = 1.0 / math.sqrt(head_dim)
    dp_count = lax.axis_size("dp")
    normalized_input = rms_rows(
        hidden_in.astype(jnp.float32), norm_gain.astype(jnp.float32)
    ).astype(jnp.bfloat16)
    piece = lax.all_gather(normalized_input, "head", axis=0, tiled=True)
    mixed = jnp.concatenate(
        [
            jnp.dot(piece, w_query, preferred_element_type=jnp.float32),
            jnp.dot(piece, key_weight, preferred_element_type=jnp.float32),
            jnp.dot(piece, w_value, preferred_element_type=jnp.float32),
        ],
        axis=1,
    )
    height = mixed.shape[0]
    segment = token_request[0]
    branch_nodes = request_node[0]
    requests = branch_nodes.shape[0]
    request_ids = jnp.arange(requests, dtype=jnp.int32)
    token_ids = jnp.arange(height, dtype=jnp.int32)
    member = segment[None, :] == request_ids[:, None]
    counts = jnp.sum(member.astype(jnp.int32), axis=1)
    earlier = request_ids[None, :] < request_ids[:, None]
    starts = jnp.sum(jnp.where(earlier, counts[None, :], 0), axis=1)
    offset = token_ids - jnp.sum(jnp.where(member, starts[:, None], 0), axis=0)
    node_total = mid_lengths.shape[0]
    node_match = branch_nodes[:, None] == jnp.arange(node_total, dtype=jnp.int32)[None, :]
    branch_length = jnp.sum(jnp.where(node_match, mid_lengths[None, :], 0), axis=1)
    root_total = prefix_root_keys.shape[0] * dp_count
    positions = (
        root_total
        + jnp.sum(jnp.where(member, (branch_length + leaf_lengths)[:, None], 0), axis=0)
        + offset
    )
    query_part = mixed[:, :query_width].reshape(height, query_width // head_dim, head_dim)
    key_portion = mixed[:, query_width : query_width + key_width].reshape(
        height, kv_heads, head_dim
    )
    query_matrix = rotate(rms_rows(query_part, query_gain.astype(jnp.float32)), positions).astype(
        jnp.bfloat16
    )
    new_keys = rotate(rms_rows(key_portion, key_gain.astype(jnp.float32)), positions).astype(
        jnp.bfloat16
    )
    new_values = mixed[:, query_width + key_width :].astype(jnp.bfloat16)
    heads_query = query_matrix.reshape(height, kv_heads, query_group, head_dim)
    root_keys = lax.all_gather(prefix_root_keys, "dp", axis=0, tiled=True)
    root_values = lax.all_gather(prefix_root_values, "dp", axis=0, tiled=True)
    owner_of = branch_nodes // MID_DEV
    owner_ids = jnp.arange(dp_count, dtype=jnp.int32)
    owner_match = owner_of[None, :] == owner_ids[:, None]
    block_slot = jnp.sum(jnp.where(owner_match, (branch_nodes % MID_DEV)[None, :], 0), axis=1)
    block_request = jnp.sum(jnp.where(owner_match, request_ids[None, :], 0), axis=1)
    block_length = jnp.sum(jnp.where(owner_match, branch_length[None, :], 0), axis=1)
    wanted = lax.all_to_all(block_slot[:, None], "dp", split_axis=0, concat_axis=0, tiled=True)[
        :, 0
    ]
    second = (wanted == 1)[:, None, None]
    own_pairs = jnp.concatenate([mid_keys, mid_values], axis=1).reshape(
        MID_DEV, MID_LEN, 2 * key_width
    )
    sent = jnp.where(second, own_pairs[1][None], own_pairs[0][None])
    got = lax.all_to_all(sent, "dp", split_axis=0, concat_axis=0, tiled=True)
    got = got.reshape(dp_count * MID_LEN, 2 * key_width)
    leaf_each = leaf_keys.shape[0] // requests
    leaf_live = jnp.arange(leaf_each, dtype=jnp.int32)[None, :] < leaf_lengths[:, None]
    leaf_tag = jnp.where(leaf_live, request_ids[:, None], -1).reshape(-1)
    mid_live = jnp.arange(MID_LEN, dtype=jnp.int32)[None, :] < block_length[:, None]
    mid_tag = jnp.where(mid_live, block_request[:, None], -1).reshape(-1)
    own_mask = (segment[None, :] == segment[:, None]) & (token_ids[None, :] <= token_ids[:, None])
    mask = jnp.concatenate(
        [
            jnp.ones((height, root_keys.shape[0]), jnp.bool_),
            leaf_tag[None, :] == segment[:, None],
            own_mask,
            mid_tag[None, :] == segment[:, None],
        ],
        axis=1,
    )
    all_keys = jnp.concatenate(
        [root_keys, leaf_keys, new_keys.reshape(height, key_width), got[:, :key_width]], axis=0
    ).reshape(-1, kv_heads, head_dim)
    all_values = jnp.concatenate(
        [root_values, leaf_values, new_values, got[:, key_width:]], axis=0
    ).reshape(-1, kv_heads, head_dim)
    scores = jnp.einsum(
        "tkgd,skd->kgts", heads_query, all_keys, preferred_element_type=jnp.float32
    )
    scores = jnp.where(mask[None, None], scores * scale, MASKED)
    weights = jnp.exp(scores - jnp.max(scores, axis=-1, keepdims=True))
    total = jnp.sum(weights, axis=-1)
    summed = jnp.einsum(
        "kgts,skd->kgtd",
        weights.astype(jnp.bfloat16),
        all_values,
        preferred_element_type=jnp.float32,
    )
    attn = (summed / total[..., None]).astype(jnp.bfloat16)
    attn = attn.transpose(2, 0, 1, 3).reshape(height, query_width)
    update = lax.psum_scatter(
        jnp.dot(attn, w_out, preferred_element_type=jnp.float32).astype(jnp.bfloat16),
        "head",
        scatter_dimension=0,
        tiled=True,
    )
    return (update, new_keys.reshape(height, key_width), new_values)


def solution(mesh):
    in_specs = (
        P(("dp", "head"), None),
        P(),
        P(None, "head"),
        P(None, "head"),
        P(None, "head"),
        P(),
        P(),
        P("head", None),
        P("dp", "head"),
        P("dp", "head"),
        P("dp", "head"),
        P("dp", "head"),
        P(),
        P("dp", "head"),
        P("dp", "head"),
        P("dp"),
        P("dp", None),
        P("dp", None),
    )
    out_specs = (P(("dp", "head"), None), P("dp", "head"), P("dp", "head"))
    return jax.shard_map(body, mesh=mesh, in_specs=in_specs, out_specs=out_specs, check_vma=False)
```

time: 227 us -> 208 us (0.916)
  local copies, waits for them, and re-layouts: 50.7 us -> 22.5 us
  waiting for transfers between devices: 37.2 us -> 54.8 us
  starting transfers between devices: 19 us -> 11.7 us
    gather x19 -> x0, local copies, waits for them, and re-layouts: 26.3 us -> none  [the longest x2 5.41 us: body(): jnp.take(req_summed.reshape(requests * capacity, kv_heads, query_group, h...]
    all_to_all x2 -> x1, waiting for transfers between devices: 0.01 us -> 25.7 us  [body(): got = lax.all_to_all(sent, 'dp', split_axis=0, concat_axis=0, tiled=True)]
    reduce_scatter x1, waiting for transfers between devices: 37.2 us -> 29 us  [body(): lax.psum_scatter(jnp.dot(attn, w_out, preferred_element_type=jnp.float32)...]
    all_to_all x2 -> x1, starting transfers between devices: 13.2 us -> 5.97 us  [body(): got = lax.all_to_all(sent, 'dp', split_axis=0, concat_axis=0, tiled=True)]
    concatenate x1 -> x2, other arithmetic: 1.05 us -> 8.24 us  [the longest x1 6.99 us: body(): jnp.concatenate([jnp.ones((height, root_keys.shape[0]), jnp.bool_), leaf_...]
    reshape x5 -> x1, local copies, waits for them, and re-layouts: 7.5 us -> 1.86 us  [body(): got = got.reshape(dp_count * MID_LEN, 2 * key_width)]
    slice x0 -> x4, local copies, waits for them, and re-layouts: none -> 5.57 us  [the longest x3 4.43 us: body(): sent = jnp.where(second, own_pairs[1][None], own_pairs[0][None])]
    concatenate x0 -> x5, local copies, waits for them, and re-layouts: none -> 5.1 us  [the longest x3 4.12 us: body(): jnp.concatenate([root_keys, leaf_keys, new_keys.reshape(height, key_width...]
  transfers between devices with their start and end apart: 5 -> 4, of which waited for: 1 -> 2; matrix products, arithmetic and copies ran while one was open for 38% -> 20% of each run, Pallas kernels for 0% -> 0%
where the time goes in v1:
time: 208 us; the launch traced here: 205 us
  waiting for transfers between devices  54.8 us (26%)
  blocking collectives  45.6 us (22%)
  other arithmetic  31.6 us (15%)
  matrix products  24.6 us (12%)
  local copies, waits for them, and re-layouts  22.5 us (11%)
  between operations  14.4 us (7%)
  starting transfers between devices  11.7 us (6%)
    reduce_scatter x1, waiting for transfers between devices, body(): lax.psum_scatter(jnp.dot(attn, w_out, preferred_element_type=jnp.float32)...  29 us
    all_to_all x1, waiting for transfers between devices, body(): got = lax.all_to_all(sent, 'dp', split_axis=0, concat_axis=0, tiled=True)  25.7 us
    all_gather x1, blocking collectives, body(): root_values = lax.all_gather(prefix_root_values, 'dp', axis=0, tiled=True)  23.4 us
    all_gather x1, blocking collectives, body(): root_keys = lax.all_gather(prefix_root_keys, 'dp', axis=0, tiled=True)  22.2 us
    dot_general x1, matrix products, body(): jnp.einsum('tkgd,skd->kgts', heads_query, all_keys, preferred_element_typ...  10.1 us
    reduce_sum x1, other arithmetic, body(): total = jnp.sum(weights, axis=-1)  9.09 us
    dot_general x1, matrix products, body(): jnp.einsum('kgts,skd->kgtd', weights.astype(jnp.bfloat16), all_values, pr...  7.7 us
    concatenate x1, other arithmetic, body(): jnp.concatenate([jnp.ones((height, root_keys.shape[0]), jnp.bool_), leaf_...  6.99 us
  transfers between devices with their start and end apart: 4, of which 2 were waited for; matrix products, arithmetic and copies ran while one was open for 20% of the time, Pallas kernels for 0%

profile of v1, /device:TPU:9, one launch (start us, length us, event | category | flops | bytes accessed | tf_op | source)
XLA Modules:
  0.0 205.2 jit_solution(16049318135466380190)
XLA Ops:
  9.7 5.7 %all-to-all-start = ((s32[8,1,1]{2,1,0:T(1,128)}), s32[8,1,1]{2,1,0:T(1,128)S(1)}, u32[]{:S(2)}, u32[]{:S(2)}) async-start(s32[8,1,1]{2,1,0:T(1,128)} %copy.122), calls=%async_computation | async-start | bytes 8192 | tf_op jit(solution)/shard_map/all_to_all | solution.py:116
  17.2 1.8 fusion.24
  24.2 23.4 %all_gather.11 = bf16[1024,256]{0,1:T(8,128)(2,1)} all-gather(bf16[128,256]{0,1:T(8,128)(2,1)S(1)} %copy.133), channel_id=1, replica_groups=mesh['dp'=8,'head'=4] {'dp'}, dimensions={0}, use_global_device_ids=true | all-gather | bytes 589824 | tf_op jit(solution)/shard_map/all_gather | solution.py:109
  48.5 22.2 %all_gather.9 = bf16[1024,256]{0,1:T(8,128)(2,1)S(1)} all-gather(bf16[128,256]{0,1:T(8,128)(2,1)S(1)} %copy.119), channel_id=1, replica_groups=mesh['dp'=8,'head'=4] {'dp'}, dimensions={0}, use_global_device_ids=true | all-gather | bytes 589824 | tf_op jit(solution)/shard_map/all_gather | solution.py:108
  71.6 1.8 copy.124
  73.4 1.8 copy.123
  75.2 1.8 copy.134
  78.3 1.8 copy.120
  80.1 1.8 copy.127
  83.1 2.7 %broadcast_select_fusion = bf16[8,256,512]{1,2,0:T(8,128)(2,1)} fusion(pred[8]{0:T(512)(128)(4,1)S(1)} %compare_reduce_fusion, bf16[256,512]{0,1:T(8,128)(2,1)} %copy.124, bf16[256,512]{0,1:T(8,128)(2,1)} %copy.123), kind=kLoop, calls=%fused_computation.9 | loop fusion | flops 1048576 | bytes 2621448 | tf_op jit(solution)/shard_map/jit(_where)/select_n | solution.py:123
  85.8 6.0 %all-to-all-start.1 = ((bf16[8,256,512]{1,2,0:T(8,128)(2,1)}), bf16[8,256,512]{1,2,0:T(8,128)(2,1)}, u32[]{:S(2)}, u32[]{:S(2)}) async-start(bf16[8,256,512]{1,2,0:T(8,128)(2,1)} %broadcast_select_fusion), calls=%async_computation.1 | async-start | bytes 4194304 | tf_op jit(solution)/shard_map/all_to_all | solution.py:124
  91.9 7.0 %pad_add_fusion = pred[256,3840]{0,1:T(8,128)(4,1)} fusion(pred[256,2048]{0,1:T(8,128)(4,1)S(1)} %broadcast_compare_fusion, pred[256,256]{0,1:T(8,128)(4,1)S(1)} %fusion.28, pred[256,512]{0,1:T(8,128)(4,1)S(1)} %broadcast_compare_fusion.1, pred[3840]{0:T(1024)(128)(4,1)S(1)} %pad.8.clone), kind=kLoop, calls=%fused_computation.7 | loop fusion | flops 2949120 | bytes 1707776 | tf_op jit(solution)/shard_map/concatenate | solution.py:132
  98.9 2.0 convolution_convert_fusion.1
  101.6 2.6 %fusion.36 = f32[256,512]{1,0:T(8,128)S(1)} fusion(bf16[256,2048]{1,0:T(8,128)(2,1)} %all-gather.2.cloned.1.call-done, bf16[2048,512]{1,0:T(8,128)(2,1)} %param.20), kind=kOutput, calls=%fused_computation.82 | convolution fusion | flops 536870912 | bytes 3670016 | tf_op jit(solution)/shard_map/dot_general | solution.py:70
  108.3 25.7 %all-to-all-done.1 = bf16[8,256,512]{1,2,0:T(8,128)(2,1)} async-done(((bf16[8,256,512]{1,2,0:T(8,128)(2,1)}), bf16[8,256,512]{1,2,0:T(8,128)(2,1)}, u32[]{:S(2)}, u32[]{:S(2)}) %all-to-all-start.1) | async-done | bytes 2097184 | tf_op jit(solution)/shard_map/all_to_all | solution.py:124
  134.1 1.9 copy.142
  136.0 1.1 fusion.34
  137.1 1.3 copy.128
  138.4 10.1 %fusion.2 = (f32[2,2,256]{2,1,0:T(2,128)S(1)}, f32[2,3840,256,2]{2,1,3,0:T(8,128)}) fusion(pred[256,3840]{0,1:T(8,128)(4,1)} %pad_add_fusion, bf16[256,2,2,64]{3,0,2,1:T(8,128)(2,1)} %bitcast.71, bf16[256,2,2,64]{3,0,2,1:T(8,128)(2,1)} %bitcast.72, bf16[2048,2,128]{2,0,1:T(8,128)(2,1)} %copy.128, bf16[256,2,128]{2,0,1:T(8,128)(2,1)S(1)} %maximum_convert_fusion, ...), kind=kOutput, calls=%fused_computation.4 | convolution fusion | flops 1026817024 | bytes 18944000 | tf_op jit(solution)/shard_map/tkgd,skd->kgts/dot_general | solution.py:147
  148.5 9.1 %fusion = f32[2,2,256]{2,1,0:T(2,128)S(1)} fusion(f32[2,3840,256,2]{2,1,3,0:T(8,128)} %get-tuple-element.41, f32[2,2,256]{2,1,0:T(2,128)S(1)} %get-tuple-element.40, pred[256,3840]{0,1:T(8,128)(4,1)} %pad_add_fusion), kind=kLoop, calls=%fused_computation.2 | loop fusion | flops 15727616 | bytes 16719872 | tf_op jit(solution)/shard_map/reduce_sum | solution.py:152
  157.6 1.2 pad_maximum_fusion
  158.9 7.7 %fusion.19 = bf16[256,2,2,128]{0,3,2,1:T(8,128)(2,1)S(1)} fusion(bf16[3840,2,128,1]{0,2,3,1:T(8,128)(2,1)S(1)} %bitcast.67, f32[2,3840,256,2]{2,1,3,0:T(8,128)} %get-tuple-element.41, f32[2,2,256]{2,1,0:T(2,128)S(1)} %get-tuple-element.40, pred[256,3840]{0,1:T(8,128)(4,1)S(1)} %copy-done.3, f32[256,2,2]{0,2,1:T(2,128)S(1)} %bitcast.80), kind=kOutput, calls=%fused_computation.22 | convolution fusion | flops 1022623744 | bytes 18948096 | tf_op jit(solution)/shard_map/kgts,skd->kgtd/dot_general | solution.py:153
  166.7 1.7 convolution_convert_fusion
  169.3 29.0 %reduce-scatter.2.cloned.1.call-done = bf16[64,2048]{1,0:T(8,128)(2,1)} async-done(((bf16[256,2048]{1,0:T(8,128)(2,1)}), bf16[64,2048]{1,0:T(8,128)(2,1)}) %reduce-scatter.2.cloned.1.call-update) | async-done | bytes 262160 | tf_op jit(solution)/shard_map/reduce_scatter | solution.py:161
  (80 shorter events, 19.6 us)
Async XLA Ops:
  7.2 159.5 %copy-start = (bf16[512,2048]{1,0:T(8,128)(2,1)S(1)}, bf16[512,2048]{1,0:T(8,128)(2,1)}, u32[]{:S(2)}) copy-start(bf16[512,2048]{1,0:T(8,128)(2,1)} %param.25) | copy-start | bytes 6291460
  7.2 40.5 %copy-start.12 = (s32[1,256]{1,0:T(1,128)S(1)}, s32[1,256]{1,0:T(1,128)}, u32[]{:S(2)}) copy-start(s32[1,256]{1,0:T(1,128)} %param.34) | copy-start | bytes 3076
  7.2 41.2 %copy-start.11 = (bf16[128,256]{1,0:T(8,128)(2,1)S(1)}, bf16[128,256]{1,0:T(8,128)(2,1)}, u32[]{:S(2)}) copy-start(bf16[128,256]{1,0:T(8,128)(2,1)} %param.26) | copy-start | bytes 196612
  9.7 73.2 %all-to-all-start = ((s32[8,1,1]{2,1,0:T(1,128)}), s32[8,1,1]{2,1,0:T(1,128)S(1)}, u32[]{:S(2)}, u32[]{:S(2)}) async-start(s32[8,1,1]{2,1,0:T(1,128)} %copy.122), calls=%async_computation | async-start | bytes 8192 | tf_op jit(solution)/shard_map/all_to_all | solution.py:116
  15.4 83.5 %all-gather.2.cloned.1.call-start = ((), (), s32[]{:S(2)}) async-start(), calls=%async_computation.3 | async-start | bytes 1310720 | tf_op jit(solution)/shard_map/all_gather | solution.py:67
  85.8 48.3 %all-to-all-start.1 = ((bf16[8,256,512]{1,2,0:T(8,128)(2,1)}), bf16[8,256,512]{1,2,0:T(8,128)(2,1)}, u32[]{:S(2)}, u32[]{:S(2)}) async-start(bf16[8,256,512]{1,2,0:T(8,128)(2,1)} %broadcast_select_fusion), calls=%async_computation.1 | async-start | bytes 4194304 | tf_op jit(solution)/shard_map/all_to_all | solution.py:124
  91.8 106.6 %reduce-scatter.2.cloned.1.call-start = ((), (), s32[]{:S(2)}) async-start(), calls=%async_computation.4 | async-start | bytes 1310720 | tf_op jit(solution)/shard_map/reduce_scatter | solution.py:161
  100.9 4.9 %copy-start.6 = (bf16[256,256]{1,0:T(8,128)(2,1)}, bf16[256,256]{1,0:T(8,128)(2,1)S(1)}, u32[]{:S(2)}) copy-start(bf16[256,256]{1,0:T(8,128)(2,1)S(1)} %convolution_convert_fusion.1) | copy-start | bytes 393220
  104.4 2.8 %copy-start.1 = (bf16[256,2048]{1,0:T(8,128)(2,1)S(1)}, bf16[256,2048]{1,0:T(8,128)(2,1)}, u32[]{:S(2)}) copy-start(bf16[256,2048]{1,0:T(8,128)(2,1)} %all-gather.2.cloned.1.call-done) | copy-start | bytes 3145732
  104.5 2.8 %copy-start.4 = (bf16[2048,256]{1,0:T(8,128)(2,1)S(1)}, bf16[2048,256]{1,0:T(8,128)(2,1)}, u32[]{:S(2)}) copy-start(bf16[2048,256]{1,0:T(8,128)(2,1)} %param.21) | copy-start | bytes 3145732
  108.3 30.1 %copy-start.8 = (bf16[256,2,128]{2,0,1:T(8,128)(2,1)}, bf16[256,2,128]{2,0,1:T(8,128)(2,1)S(1)}, u32[]{:S(2)}) copy-start(bf16[256,2,128]{2,0,1:T(8,128)(2,1)S(1)} %maximum_convert_fusion) | copy-start | bytes 393220
  136.0 2.5 %copy-start.10 = (bf16[512,2,128]{2,0,1:T(8,128)(2,1)S(1)}, bf16[512,2,128]{2,0,1:T(8,128)(2,1)}, u32[]{:S(2)}) copy-start(bf16[512,2,128]{2,0,1:T(8,128)(2,1)} %copy.127) | copy-start | bytes 786436
  148.5 9.1 %copy-start.2 = (bf16[2048,256]{0,1:T(8,128)(2,1)S(1)}, bf16[2048,256]{0,1:T(8,128)(2,1)}, u32[]{:S(2)}) copy-start(bf16[2048,256]{0,1:T(8,128)(2,1)} %get-tuple-element.27) | copy-start | bytes 3145732
  148.5 9.1 %copy-start.5 = (bf16[512,256]{0,1:T(8,128)(2,1)S(1)}, bf16[512,256]{0,1:T(8,128)(2,1)}, u32[]{:S(2)}) copy-start(bf16[512,256]{0,1:T(8,128)(2,1)} %copy.134) | copy-start | bytes 786436
  148.5 9.1 %copy-start.7 = (bf16[256,256]{0,1:T(8,128)(2,1)S(1)}, bf16[256,256]{0,1:T(8,128)(2,1)}, u32[]{:S(2)}) copy-start(bf16[256,256]{0,1:T(8,128)(2,1)} %copy.135) | copy-start | bytes 393220
  157.6 1.4 copy-start.3
  166.7 1.8 copy-start.9
Sparse Core Ops, SparseCore 0:
  19.2 18.5 all-gather.1
  168.5 29.7 reduce-scatter.1

commit v2 on v1

v2 whole, which is shorter than its diff:
```python
import functools
import math

import jax
import jax.numpy as jnp
import numpy as np
from jax import lax
from jax.experimental import pallas as pl
from jax.experimental.pallas import tpu as pltpu
from jax.sharding import PartitionSpec as P

MID_DEV = 2
MID_LEN = 256
EPS = 1e-06
THETA = 1000000.0
MASKED = -1e30
F32 = jnp.float32
BF16 = jnp.bfloat16
MESH = pl.DeviceIdType.MESH


def kernel(
    n_dp, n_head,
    hidden, norm_gain, wq_hbm, wk_hbm, wv_hbm, query_gain, key_gain, wo_hbm, root_k, root_v,
    mid_k, mid_v, mid_len, leaf_k, leaf_v, leaf_len, seg_in, node_in, freqs,
    out, new_k, new_v,
    wq, wk, wv, wo, normed, info, roots_k, roots_v, staged, mids, queries, tags, top, acc, attn,
    parts, got, local_sem, hid_send, hid_recv, info_send, info_recv, rk_send, rk_recv, rv_send,
    rv_recv, mid_send, mid_recv, part_send, part_recv,
):
    me, mh = lax.axis_index("dp"), lax.axis_index("head")
    share = hidden.shape[0]
    height = normed.shape[0]
    requests = node_in.shape[1]
    nodes = mid_len.shape[1]
    root_rows = root_k.shape[0]
    kv_heads = wk.shape[1] // 128
    group = wq.shape[1] // wk.shape[1]
    kw = wk.shape[1]
    scale = 1.0 / math.sqrt(128)

    loads = [
        pltpu.make_async_copy(a, b, local_sem.at[i])
        for i, (a, b) in enumerate(((wq_hbm, wq), (wk_hbm, wk), (wv_hbm, wv), (wo_hbm, wo)))
    ]
    for load in loads:
        load.start()

    barrier = pltpu.get_barrier_semaphore()

    def greet_dp(d, _):
        pl.semaphore_signal(
            barrier, inc=1, device_id=(lax.rem(me + d, n_dp), mh), device_id_type=MESH
        )
        return 0

    def greet_head(d, _):
        pl.semaphore_signal(
            barrier, inc=1, device_id=(me, lax.rem(mh + d, n_head)), device_id_type=MESH
        )
        return 0

    lax.fori_loop(1, n_dp, greet_dp, 0)
    lax.fori_loop(1, n_head, greet_head, 0)

    x = hidden[...].astype(F32)
    power = jnp.mean(x * x, axis=-1, keepdims=True)
    x = (x * lax.rsqrt(power + EPS) * norm_gain[...].astype(F32)).astype(BF16)
    my_rows = pl.ds(pl.multiple_of(mh * share, share), share)
    normed[my_rows, :] = x

    eye = lax.broadcasted_iota(jnp.int32, (requests, requests), 0) == lax.broadcasted_iota(
        jnp.int32, (requests, requests), 1
    )

    def column(row):
        return jnp.sum(jnp.where(eye, row.astype(F32), 0.0), axis=1, keepdims=True)

    branch = column(node_in[...])
    info[me] = jnp.broadcast_to(branch, (requests, 128))
    my_root = pl.ds(pl.multiple_of(me * root_rows, root_rows), root_rows)
    roots_k[my_root, :] = root_k[...]
    roots_v[my_root, :] = root_v[...]

    pl.semaphore_wait(barrier, n_dp + n_head - 2)

    def hid_copy(d, source):
        rows = pl.ds(pl.multiple_of(source * share, share), share)
        return pltpu.make_async_remote_copy(
            normed.at[rows, :], normed.at[rows, :], hid_send.at[d], hid_recv.at[source],
            device_id=(me, lax.rem(mh + d, n_head)), device_id_type=MESH,
        )

    def info_copy(d, source):
        return pltpu.make_async_remote_copy(
            info.at[source], info.at[source], info_send.at[d], info_recv.at[source],
            device_id=(lax.rem(me + d, n_dp), mh), device_id_type=MESH,
        )

    def root_copies(d, source):
        rows = pl.ds(pl.multiple_of(source * root_rows, root_rows), root_rows)
        target = (lax.rem(me + d, n_dp), mh)
        return (
            pltpu.make_async_remote_copy(
                roots_k.at[rows, :], roots_k.at[rows, :], rk_send.at[d], rk_recv.at[source],
                device_id=target, device_id_type=MESH,
            ),
            pltpu.make_async_remote_copy(
                roots_v.at[rows, :], roots_v.at[rows, :], rv_send.at[d], rv_recv.at[source],
                device_id=target, device_id_type=MESH,
            ),
        )

    def mid_copy(d, source):
        return pltpu.make_async_remote_copy(
            staged.at[d], mids.at[source], mid_send.at[d], mid_recv.at[source],
            device_id=(lax.rem(me + d, n_dp), mh), device_id_type=MESH,
        )

    def part_copy(d, source):
        return pltpu.make_async_remote_copy(
            parts.at[d], got.at[source], part_send.at[d], part_recv.at[source],
            device_id=(me, lax.rem(mh + d, n_head)), device_id_type=MESH,
        )

    def over(count, act):
        def step(d, _):
            act(d)
            return 0

        lax.fori_loop(1, count, step, 0)

    over(n_dp, lambda d: info_copy(d, me).start())
    over(n_head, lambda d: hid_copy(d, mh).start())

    def send_root(d):
        for copy in root_copies(d, me):
            copy.start()

    over(n_dp, send_root)

    def chosen(who):
        wish = jnp.max(jnp.where(info[who] == (MID_DEV * me + 1).astype(F32), 1.0, 0.0), axis=0, keepdims=True)
        wish = jnp.max(wish, axis=1, keepdims=True)
        pair = [
            jnp.concatenate([mid_k[pl.ds(s * MID_LEN, MID_LEN), :], mid_v[pl.ds(s * MID_LEN, MID_LEN), :]], axis=1).astype(F32)
            for s in range(2)
        ]
        wide = jnp.broadcast_to(wish, pair[0].shape)
        return jnp.where(wide > 0.5, pair[1], pair[0]).astype(BF16)

    def send_mid(d):
        who = lax.rem(me + d, n_dp)
        info_copy(d, who).wait_recv()
        staged[d] = chosen(who)
        mid_copy(d, me).start()

    over(n_dp, send_mid)
    mids[me] = chosen(me)

    seg = seg_in[...].astype(F32)
    req = lax.broadcasted_iota(jnp.int32, (requests, height), 0).astype(F32)
    starts = jnp.sum(jnp.where(seg < req, 1.0, 0.0), axis=1, keepdims=True)
    node_ids = lax.broadcasted_iota(jnp.int32, (requests, nodes), 1).astype(F32)
    branch_len = jnp.sum(
        jnp.where(node_ids == branch, mid_len[...].astype(F32), 0.0), axis=1, keepdims=True
    )
    leaf_col = column(leaf_len[...])
    base = root_rows * n_dp + branch_len + leaf_col - starts
    pos = jnp.sum(jnp.where(seg == req, base, 0.0), axis=0, keepdims=True)
    pos = pos + lax.broadcasted_iota(jnp.int32, (1, height), 1).astype(F32)
    pos = jnp.transpose(jnp.broadcast_to(pos, (128, height)))
    seg_rep = jnp.transpose(jnp.broadcast_to(seg, (128, height)))
    lane = lax.broadcasted_iota(jnp.int32, (height, 128), 1)
    tags[...] = jnp.where(seg_rep == lane.astype(F32), 1.0, 0.0).astype(BF16)
    spread = lax.broadcasted_iota(jnp.int32, (requests, 128), 0) == lax.broadcasted_iota(
        jnp.int32, (requests, 128), 1
    )

    def lanes(col):
        return jnp.sum(jnp.where(spread, col, 0.0), axis=0, keepdims=True)

    real = jnp.sum(jnp.where(spread, 1.0, 0.0), axis=0, keepdims=True)
    leaf_row, mid_row, node_row = lanes(leaf_col), lanes(branch_len), lanes(branch)
    node_row = jnp.where(real > 0.5, node_row, -2.0)
    angle = pos * freqs[...]
    cosine = jnp.cos(angle)
    sine = jnp.sin(angle)
    sine = jnp.where(lane < 64, -sine, sine)

    over(n_head, lambda d: hid_copy(d, lax.rem(mh + d, n_head)).wait_recv())
    for load in loads:
        load.wait()
    inputs = normed[...]
    values = jnp.dot(inputs, wv[...], preferred_element_type=F32).astype(BF16)
    new_v[...] = values

    def turned(y, gain):
        power = jnp.mean(y * y, axis=-1, keepdims=True)
        y = y * lax.rsqrt(power + EPS) * gain[...].astype(F32)
        return (y * cosine + pltpu.roll(y, 64, axis=1) * sine).astype(BF16)

    for j in range(kv_heads):
        cols = slice(j * 128, j * 128 + 128)
        y = jnp.dot(inputs, wk[:, cols], preferred_element_type=F32)
        new_k[:, cols] = turned(y, key_gain)
    for j in range(kv_heads):
        for g in range(group):
            h = j * group + g
            y = jnp.dot(inputs, wq[:, h * 128 : h * 128 + 128], preferred_element_type=F32)
            queries[j, g * height : (g + 1) * height, :] = turned(y, query_gain)

    tall = group * height

    def attend(j, keys, bias, vals, first=False, causal=False):
        q = queries[j]
        if bias is not None:
            q = jnp.concatenate([q, jnp.concatenate([tags[...]] * group, axis=0)], axis=1)
            keys = jnp.concatenate([keys, bias], axis=1)
        s = lax.dot_general(q, keys, (((1,), (1,)), ((), ())), preferred_element_type=F32)
        if causal:
            row = lax.broadcasted_iota(jnp.int32, (tall, height), 0) % height
            s = jnp.where(lax.broadcasted_iota(jnp.int32, (tall, height), 1) <= row, s, MASKED)
        peak = jnp.max(s, axis=1, keepdims=True)
        if not first:
            old = top[j]
            peak = jnp.maximum(old[:, :1], peak)
        p = jnp.exp((s - peak) * scale).astype(BF16)
        wide = jnp.concatenate([vals, jnp.ones((vals.shape[0], 128), BF16)], axis=1)
        r = jnp.dot(p, wide, preferred_element_type=F32)
        full = jnp.broadcast_to(peak, (tall, 128))
        if not first:
            shrink = jnp.exp((old - full) * scale)
            r = acc[j] * jnp.concatenate([shrink, shrink], axis=1) + r
        acc[j] = r
        top[j] = full

    key_row = lax.broadcasted_iota(jnp.int32, (height, 128), 0)
    own_bias = jnp.where(tags[...].astype(F32) > 0.5, 0.0, MASKED).astype(BF16)
    for j in range(kv_heads):
        cols = slice(j * 128, j * 128 + 128)
        attend(j, new_k[:, cols], own_bias, new_v[:, cols], first=True, causal=True)
    leaf_each = leaf_k.shape[0] // requests

    def leaf_step(i, _):
        rows = pl.ds(pl.multiple_of(i * 256, 256), 256)
        at = lax.broadcasted_iota(jnp.int32, (256, 128), 0) + i * 256
        mine = lax.broadcasted_iota(jnp.int32, (256, 128), 1) == at // leaf_each
        live = (at % leaf_each).astype(F32) < leaf_row
        bias = jnp.where(mine & live, 0.0, MASKED).astype(BF16)
        for j in range(kv_heads):
            cols = slice(j * 128, j * 128 + 128)
            attend(j, leaf_k[rows, cols], bias, leaf_v[rows, cols])
        return 0

    lax.fori_loop(0, leaf_k.shape[0] // 256, leaf_step, 0)

    def mid_block(who):
        at = lax.broadcasted_iota(jnp.int32, (MID_LEN, 128), 0).astype(F32)
        first_node = (MID_DEV * who).astype(F32)
        mine = (node_row >= first_node) & (node_row < first_node + MID_DEV)
        reach = jnp.where(mine, mid_row, 0.0)
        bias = jnp.where(at < reach, 0.0, MASKED).astype(BF16)
        block = mids.at[who]
        for j in range(kv_heads):
            attend(
                j, block[:, j * 128 : j * 128 + 128], bias,
                block[:, kw + j * 128 : kw + j * 128 + 128],
            )

    mid_block(me)

    def root_wait(d):
        for copy in root_copies(d, lax.rem(me + d, n_dp)):
            copy.wait_recv()

    over(n_dp, root_wait)

    def root_step(i, _):
        rows = pl.ds(pl.multiple_of(i * 512, 512), 512)
        for j in range(kv_heads):
            cols = slice(j * 128, j * 128 + 128)
            attend(j, roots_k[rows, cols], None, roots_v[rows, cols])
        return 0

    lax.fori_loop(0, root_rows * n_dp // 512, root_step, 0)

    def mid_step(d):
        who = lax.rem(me + n_dp - d, n_dp)
        mid_copy(d, who).wait_recv()
        mid_block(who)

    over(n_dp, mid_step)

    for j in range(kv_heads):
        r = acc[j]
        y = (r[:, :128] / r[:, 128:]).astype(BF16)
        for g in range(group):
            h = j * group + g
            attn[:, h * 128 : h * 128 + 128] = y[g * height : (g + 1) * height]

    def product(who):
        rows = pl.ds(pl.multiple_of(who * share, share), share)
        return jnp.dot(attn[rows, :], wo[...], preferred_element_type=F32).astype(BF16)

    def send_part(d):
        parts[d] = product(lax.rem(mh + d, n_head))
        part_copy(d, mh).start()

    over(n_head, send_part)
    total = product(mh).astype(F32)
    for d in range(1, n_head):
        who = lax.rem(mh + d, n_head)
        part_copy(d, who).wait_recv()
        total = total + got[who].astype(F32)
    out[...] = total.astype(BF16)

    def finish_dp(d):
        info_copy(d, me).wait_send()
        for copy in root_copies(d, me):
            copy.wait_send()
        mid_copy(d, me).wait_send()

    def finish_head(d):
        hid_copy(d, mh).wait_send()
        part_copy(d, mh).wait_send()

    over(n_dp, finish_dp)
    over(n_head, finish_head)


def body(
    hidden_in, norm_gain, w_query, key_weight, w_value, query_gain, key_gain, w_out,
    prefix_root_keys, prefix_root_values, mid_keys, mid_values, mid_lengths, leaf_keys,
    leaf_values, leaf_lengths, token_request, request_node,
):
    n_dp, n_head = lax.axis_size("dp"), lax.axis_size("head")
    share, model = hidden_in.shape
    height = share * n_head
    qw, kw = w_query.shape[1], key_weight.shape[1]
    kv_heads, group = kw // 128, qw // kw
    requests = request_node.shape[1]
    root_rows = prefix_root_keys.shape[0]
    half = np.arange(64, dtype=np.float32) * np.float32(2.0 / 128)
    freqs = np.power(np.float32(THETA), -half).astype(np.float32)
    freqs = jnp.asarray(np.concatenate([freqs, freqs])[None])
    vmem = pl.BlockSpec(memory_space=pltpu.VMEM)
    hbm = pl.BlockSpec(memory_space=pl.ANY)
    dma = pltpu.SemaphoreType.DMA
    return pl.pallas_call(
        functools.partial(kernel, n_dp, n_head),
        out_shape=(
            jax.ShapeDtypeStruct((share, model), BF16),
            jax.ShapeDtypeStruct((height, kw), BF16),
            jax.ShapeDtypeStruct((height, kw), BF16),
        ),
        in_specs=[vmem, vmem, hbm, hbm, hbm, vmem, vmem, hbm] + [vmem] * 11,
        out_specs=(vmem, vmem, vmem),
        scratch_shapes=[
            pltpu.VMEM(w_query.shape, BF16),
            pltpu.VMEM(key_weight.shape, BF16),
            pltpu.VMEM(w_value.shape, BF16),
            pltpu.VMEM(w_out.shape, BF16),
            pltpu.VMEM((height, model), BF16),
            pltpu.VMEM((n_dp, requests, 128), F32),
            pltpu.VMEM((n_dp * root_rows, kw), BF16),
            pltpu.VMEM((n_dp * root_rows, kw), BF16),
            pltpu.VMEM((n_dp, MID_LEN, 2 * kw), BF16),
            pltpu.VMEM((n_dp, MID_LEN, 2 * kw), BF16),
            pltpu.VMEM((kv_heads, group * height, 128), BF16),
            pltpu.VMEM((height, 128), BF16),
            pltpu.VMEM((kv_heads, group * height, 128), F32),
            pltpu.VMEM((kv_heads, group * height, 256), F32),
            pltpu.VMEM((height, qw), BF16),
            pltpu.VMEM((n_head, share, model), BF16),
            pltpu.VMEM((n_head, share, model), BF16),
            dma((4,)),
            dma((n_head,)), dma((n_head,)),
            dma((n_dp,)), dma((n_dp,)),
            dma((n_dp,)), dma((n_dp,)),
            dma((n_dp,)), dma((n_dp,)),
            dma((n_dp,)), dma((n_dp,)),
            dma((n_head,)), dma((n_head,)),
        ],
        compiler_params=pltpu.CompilerParams(
            collective_id=0, has_side_effects=True, vmem_limit_bytes=56 * 2**20
        ),
    )(
        hidden_in, norm_gain[None], w_query, key_weight, w_value, query_gain[None],
        key_gain[None], w_out, prefix_root_keys, prefix_root_values, mid_keys, mid_values,
        mid_lengths[None], leaf_keys, leaf_values, leaf_lengths[None], token_request,
        request_node, freqs,
    )


def solution(mesh):
    shard = P("dp", "head")
    tokens = P(("dp", "head"), None)
    in_specs = (
        tokens, P(), P(None, "head"), P(None, "head"), P(None, "head"), P(), P(),
        P("head", None), shard, shard, shard, shard, P(), shard, shard, P("dp"),
        P("dp", None), P("dp", None),
    )
    return jax.shard_map(
        body, mesh=mesh, in_specs=in_specs, out_specs=(tokens, shard, shard), check_vma=False
    )
```

time: 208 us -> 101 us (0.49)
  the two profiles are of different devices: /device:TPU:9 before, /device:TPU:29 now
where the time goes in v2:
time: 101 us; the launch traced here: 100 us
  Pallas kernels  93.6 us (93%)
  local copies, waits for them, and re-layouts  6.1 us (6%)
    pallas_call x1, Pallas kernels, body(): pl.pallas_call(functools.partial(kernel, n_dp, n_head), out_shape=(jax.Sh...  93.6 us
    unnamed x3, local copies, waits for them, and re-layouts  4.8 us

profile of v2, /device:TPU:29, one launch (start us, length us, event | category | flops | bytes accessed | tf_op | source)
XLA Modules:
  0.0 100.3 jit_solution(2835572769672635132)
XLA Ops:
  0.6 1.3 %broadcast_in_dim.15.norm_gain = bf16[1,2048]{1,0:T(2,128)(2,1)} reshape(bf16[2048]{0:T(1024)(128)(2,1)} %param.20) | data formatting | bytes 8192 | tf_op jit(solution)/shard_map/broadcast_in_dim | solution.py:389
  1.9 93.6 %shard_map.202 = (bf16[64,2048]{1,0:T(8,128)(2,1)}, bf16[256,256]{1,0:T(8,128)(2,1)}, bf16[256,256]{1,0:T(8,128)(2,1)}) custom-call(bf16[64,2048]{1,0:T(8,128)(2,1)} %hidden.1, bf16[1,2048]{1,0:T(2,128)(2,1)} %broadcast_in_dim.15.norm_gain, bf16[2048,512]{1,0:T(8,128)(2,1)} %wq_hbm.1, bf16[2048,256]{1,0:T(8,128)(2,1)} %wk_hbm.1, bf16[2048,256]{1,0:T(8,128)(2,1)} %wv_hbm.1, ...), custom_call_target="tpu_custom_call" | custom-call | tf_op jit(solution)/shard_map/pallas_call | solution.py:350
  95.5 1.7 %copy.25 = bf16[64,2048]{1,0:T(8,128)(2,1)} copy(bf16[64,2048]{1,0:T(8,128)(2,1)} %get-tuple-element.6) | data formatting | bytes 524288
  97.2 1.6 %copy.26 = bf16[256,256]{1,0:T(8,128)(2,1)} copy(bf16[256,256]{1,0:T(8,128)(2,1)} %get-tuple-element.7) | data formatting | bytes 262144
  98.8 1.6 %copy.27 = bf16[256,256]{1,0:T(8,128)(2,1)} copy(bf16[256,256]{1,0:T(8,128)(2,1)} %get-tuple-element.8) | data formatting | bytes 262144

commit v3 on v2

--- a/solution.py
+++ b/solution.py
@@ -97,19 +97,33 @@
             device_id=(lax.rem(me + d, n_dp), mh), device_id_type=MESH,
         )
 
-    def root_copies(d, source):
-        rows = pl.ds(pl.multiple_of(source * root_rows, root_rows), root_rows)
-        target = (lax.rem(me + d, n_dp), mh)
-        return (
+    def flipped(d):
+        other = me
+        for k in range(n_dp.bit_length() - 1):
+            if d >> k & 1:
+                other = other + (1 - 2 * lax.rem(me // 2**k, 2)) * 2**k
+        return other
+
+    def root_copies(d, block):
+        low = d & -d
+        rows = pl.ds(pl.multiple_of(block * root_rows, root_rows), root_rows)
+        target = (flipped(low), mh)
+        return [
             pltpu.make_async_remote_copy(
-                roots_k.at[rows, :], roots_k.at[rows, :], rk_send.at[d], rk_recv.at[source],
+                held.at[rows, :], held.at[rows, :], send.at[d], recv.at[d],
                 device_id=target, device_id_type=MESH,
-            ),
-            pltpu.make_async_remote_copy(
-                roots_v.at[rows, :], roots_v.at[rows, :], rv_send.at[d], rv_recv.at[source],
-                device_id=target, device_id_type=MESH,
-            ),
-        )
+            )
+            for held, send, recv in ((roots_k, rk_send, rk_recv), (roots_v, rv_send, rv_recv))
+        ]
+
+    def relay(low):
+        for d in range(low, n_dp, 2 * low):
+            block = d - low
+            if block & -block == 2 * low:
+                for copy in root_copies(block, flipped(block)):
+                    copy.wait_recv()
+            for copy in root_copies(d, flipped(block)):
+                copy.start()
 
     def mid_copy(d, source):
         return pltpu.make_async_remote_copy(
@@ -133,11 +147,8 @@
     over(n_dp, lambda d: info_copy(d, me).start())
     over(n_head, lambda d: hid_copy(d, mh).start())
 
-    def send_root(d):
-        for copy in root_copies(d, me):
-            copy.start()
-
-    over(n_dp, send_root)
+    hops = [n_dp >> k for k in range(1, n_dp.bit_length())]
+    relay(hops[0])
 
     def chosen(who):
         wish = jnp.max(jnp.where(info[who] == (MID_DEV * me + 1).astype(F32), 1.0, 0.0), axis=0, keepdims=True)
@@ -157,6 +168,7 @@
 
     over(n_dp, send_mid)
     mids[me] = chosen(me)
+    relay(hops[1])
 
     seg = seg_in[...].astype(F32)
     req = lax.broadcasted_iota(jnp.int32, (requests, height), 0).astype(F32)
@@ -210,6 +222,8 @@
             y = jnp.dot(inputs, wq[:, h * 128 : h * 128 + 128], preferred_element_type=F32)
             queries[j, g * height : (g + 1) * height, :] = turned(y, query_gain)
 
+    for hop in hops[2:]:
+        relay(hop)
     tall = group * height
 
     def attend(j, keys, bias, vals, first=False, causal=False):
@@ -270,11 +284,9 @@
 
     mid_block(me)
 
-    def root_wait(d):
-        for copy in root_copies(d, lax.rem(me + d, n_dp)):
+    for d in range(1, n_dp, 2):
+        for copy in root_copies(d, flipped(d)):
             copy.wait_recv()
-
-    over(n_dp, root_wait)
 
     def root_step(i, _):
         rows = pl.ds(pl.multiple_of(i * 512, 512), 512)
@@ -317,8 +329,6 @@
 
     def finish_dp(d):
         info_copy(d, me).wait_send()
-        for copy in root_copies(d, me):
-            copy.wait_send()
         mid_copy(d, me).wait_send()
 
     def finish_head(d):
@@ -326,6 +336,9 @@
         part_copy(d, mh).wait_send()
 
     over(n_dp, finish_dp)
+    for d in range(1, n_dp):
+        for copy in root_copies(d, flipped(d - (d & -d))):
+            copy.wait_send()
     over(n_head, finish_head)
 
 

time: 101 us -> 96.3 us (0.953)
  the two profiles are of different devices: /device:TPU:29 before, /device:TPU:9 now
where the time goes in v3:
time: 96.3 us; the launch traced here: 96.1 us
  Pallas kernels  89.3 us (93%)
  local copies, waits for them, and re-layouts  6.1 us (6%)
    pallas_call x1, Pallas kernels, body(): pl.pallas_call(functools.partial(kernel, n_dp, n_head), out_shape=(jax.Sh...  89.3 us
    unnamed x3, local copies, waits for them, and re-layouts  4.8 us

profile of v3, /device:TPU:9, one launch (start us, length us, event | category | flops | bytes accessed | tf_op | source)
XLA Modules:
  0.0 96.1 jit_solution(2302162527125825747)
XLA Ops:
  0.6 1.3 %broadcast_in_dim.15.norm_gain = bf16[1,2048]{1,0:T(2,128)(2,1)} reshape(bf16[2048]{0:T(1024)(128)(2,1)} %param.20) | data formatting | bytes 8192 | tf_op jit(solution)/shard_map/broadcast_in_dim | solution.py:402
  1.9 89.3 %shard_map.202 = (bf16[64,2048]{1,0:T(8,128)(2,1)}, bf16[256,256]{1,0:T(8,128)(2,1)}, bf16[256,256]{1,0:T(8,128)(2,1)}) custom-call(bf16[64,2048]{1,0:T(8,128)(2,1)} %hidden.1, bf16[1,2048]{1,0:T(2,128)(2,1)} %broadcast_in_dim.15.norm_gain, bf16[2048,512]{1,0:T(8,128)(2,1)} %wq_hbm.1, bf16[2048,256]{1,0:T(8,128)(2,1)} %wk_hbm.1, bf16[2048,256]{1,0:T(8,128)(2,1)} %wv_hbm.1, ...), custom_call_target="tpu_custom_call" | custom-call | tf_op jit(solution)/shard_map/pallas_call | solution.py:363
  91.3 1.7 %copy.25 = bf16[64,2048]{1,0:T(8,128)(2,1)} copy(bf16[64,2048]{1,0:T(8,128)(2,1)} %get-tuple-element.6) | data formatting | bytes 524288
  92.9 1.6 %copy.26 = bf16[256,256]{1,0:T(8,128)(2,1)} copy(bf16[256,256]{1,0:T(8,128)(2,1)} %get-tuple-element.7) | data formatting | bytes 262144
  94.5 1.6 %copy.27 = bf16[256,256]{1,0:T(8,128)(2,1)} copy(bf16[256,256]{1,0:T(8,128)(2,1)} %get-tuple-element.8) | data formatting | bytes 262144

commit v4 on v3

--- a/solution.py
+++ b/solution.py
@@ -63,12 +63,6 @@
     lax.fori_loop(1, n_dp, greet_dp, 0)
     lax.fori_loop(1, n_head, greet_head, 0)
 
-    x = hidden[...].astype(F32)
-    power = jnp.mean(x * x, axis=-1, keepdims=True)
-    x = (x * lax.rsqrt(power + EPS) * norm_gain[...].astype(F32)).astype(BF16)
-    my_rows = pl.ds(pl.multiple_of(mh * share, share), share)
-    normed[my_rows, :] = x
-
     eye = lax.broadcasted_iota(jnp.int32, (requests, requests), 0) == lax.broadcasted_iota(
         jnp.int32, (requests, requests), 1
     )
@@ -145,10 +139,17 @@
         lax.fori_loop(1, count, step, 0)
 
     over(n_dp, lambda d: info_copy(d, me).start())
-    over(n_head, lambda d: hid_copy(d, mh).start())
 
     hops = [n_dp >> k for k in range(1, n_dp.bit_length())]
     relay(hops[0])
+
+    x = hidden[...].astype(F32)
+    power = jnp.mean(x * x, axis=-1, keepdims=True)
+    x = (x * lax.rsqrt(power + EPS) * norm_gain[...].astype(F32)).astype(BF16)
+    my_rows = pl.ds(pl.multiple_of(mh * share, share), share)
+    normed[my_rows, :] = x
+
+    over(n_head, lambda d: hid_copy(d, mh).start())
 
     def chosen(who):
         wish = jnp.max(jnp.where(info[who] == (MID_DEV * me + 1).astype(F32), 1.0, 0.0), axis=0, keepdims=True)

time: 96.3 us -> 96.3 us (level)
  no operation moved by 1% of the time
where the time goes in v4:
time: 96.3 us; the launch traced here: 96.1 us
  Pallas kernels  89.3 us (93%)
  local copies, waits for them, and re-layouts  6.1 us (6%)
    pallas_call x1, Pallas kernels, body(): pl.pallas_call(functools.partial(kernel, n_dp, n_head), out_shape=(jax.Sh...  89.3 us
    unnamed x3, local copies, waits for them, and re-layouts  4.8 us

profile of v4, /device:TPU:9, one launch (start us, length us, event | category | flops | bytes accessed | tf_op | source)
XLA Modules:
  0.0 96.1 jit_solution(7952701681066354654)
XLA Ops:
  0.6 1.3 %broadcast_in_dim.15.norm_gain = bf16[1,2048]{1,0:T(2,128)(2,1)} reshape(bf16[2048]{0:T(1024)(128)(2,1)} %param.20) | data formatting | bytes 8192 | tf_op jit(solution)/shard_map/broadcast_in_dim | solution.py:403
  1.9 89.3 %shard_map.202 = (bf16[64,2048]{1,0:T(8,128)(2,1)}, bf16[256,256]{1,0:T(8,128)(2,1)}, bf16[256,256]{1,0:T(8,128)(2,1)}) custom-call(bf16[64,2048]{1,0:T(8,128)(2,1)} %hidden.1, bf16[1,2048]{1,0:T(2,128)(2,1)} %broadcast_in_dim.15.norm_gain, bf16[2048,512]{1,0:T(8,128)(2,1)} %wq_hbm.1, bf16[2048,256]{1,0:T(8,128)(2,1)} %wk_hbm.1, bf16[2048,256]{1,0:T(8,128)(2,1)} %wv_hbm.1, ...), custom_call_target="tpu_custom_call" | custom-call | tf_op jit(solution)/shard_map/pallas_call | solution.py:364
  91.3 1.7 %copy.25 = bf16[64,2048]{1,0:T(8,128)(2,1)} copy(bf16[64,2048]{1,0:T(8,128)(2,1)} %get-tuple-element.6) | data formatting | bytes 524288
  92.9 1.6 %copy.26 = bf16[256,256]{1,0:T(8,128)(2,1)} copy(bf16[256,256]{1,0:T(8,128)(2,1)} %get-tuple-element.7) | data formatting | bytes 262144
  94.5 1.6 %copy.27 = bf16[256,256]{1,0:T(8,128)(2,1)} copy(bf16[256,256]{1,0:T(8,128)(2,1)} %get-tuple-element.8) | data formatting | bytes 262144
